TPU v7x, 32 devices: a whole 2x2x4 slice. The times are simulated.
32 devices in a mesh: seq: 4 (over y, core), mem: 8 (over z, x).
Axes of the slice: x: 2, y: 2, z: 4, core: 2. Of those that a mesh axis runs over, the one named last changes fastest.
Arguments:
- queries: bfloat16 [128, 64, 2048], P('mem', 'seq'), may hold values from -40 to 40
- keys: bfloat16 [32, 128, 2048], P('mem'), may hold values from -8 to 8
- values: bfloat16 [32, 128, 2048], P('mem'), may hold values from -6 to 6
- grad_out: bfloat16 [128, 64, 2048], P('mem', 'seq'), may hold values from -6 to 6
- neighbour_owner: int32 [128, 2], replicated, may hold values from 0 to 7, all different within a row; in each aligned block of 16 rows (0 to 15, 16 to 31, ...) at most 6 rows name the same one
- neighbour_row: int32 [128, 2], replicated, may hold values from 0 to 3
Outputs:
- attended: bfloat16 [128, 64, 2048], P('mem', 'seq')
- grad_queries: bfloat16 [128, 64, 2048], P('mem', 'seq')
- grad_keys: bfloat16 [32, 128, 2048], P('mem', 'seq')
- grad_values: bfloat16 [32, 128, 2048], P('mem', 'seq')
Inputs may be any that keep to these rules, and one draw needn't show every extreme that they name: `neighbour_owner`: A group's two entries lie on different shards. Among the 16 groups of one index of mem (aligned blocks of rows) at most 6 name one shard, and exactly 6 do for some shard.
All inputs are finite; a program needn't handle non-finite values.
Results may differ from a plain program's by a relative error of at most 0.015.
Values may be sent and summed in bfloat16 or wider, within the bound.
A program may use at most 128 MiB of HBM per device.

v0:
```python
import math
import jax
import jax.numpy as jnp
from jax import lax
from jax.sharding import PartitionSpec as P

HEADS = 16


def route_tables(owners, shard_cap):
    ref_count = owners.shape[1]
    same_owner = owners[:, :, None] == owners[:, None, :]
    earlier = jnp.arange(ref_count)[None, :] < jnp.arange(ref_count)[:, None]
    rank_table = jnp.sum(same_owner & earlier[None], axis=2)
    return (rank_table, owners * shard_cap + rank_table)


def place_rows(source, slot_table, slot_total):
    buffer = jnp.zeros((slot_total,) + source.shape[1:], source.dtype)
    return buffer.at[slot_table].set(source)


def per_device(queries, keys, values, grad_out, neighbour_owner, neighbour_row):
    senders = lax.axis_size("mem")
    my_index = lax.axis_index("mem")
    group_dev, token_piece, feature_count = queries.shape
    shard_rows, key_len, _ = keys.shape
    head_count = HEADS
    head_width = feature_count // head_count
    scaling = 1.0 / math.sqrt(head_width)
    ref_count = 2 * group_dev
    shard_cap = max(2, 3 * group_dev // senders)
    slot_total = senders * shard_cap
    row_total = slot_total * token_piece
    owners = neighbour_owner.reshape(senders, ref_count)
    row_ids = neighbour_row.reshape(senders, ref_count)
    rank_table, slot_all = route_tables(owners, shard_cap)
    my_slots = lax.dynamic_index_in_dim(slot_all, my_index, 0, keepdims=False)
    owner_hits = owners == my_index
    picked = owner_hits[:, :, None] & (
        rank_table[:, :, None] == jnp.arange(shard_cap)[None, None, :]
    )
    slot_valid = jnp.any(picked, axis=1).reshape(slot_total)
    slot_row = jnp.sum(jnp.where(picked, row_ids[:, :, None], 0), axis=1).reshape(slot_total)
    send_queries = place_rows(jnp.repeat(queries, 2, axis=0), my_slots, slot_total)
    send_grads = place_rows(jnp.repeat(grad_out, 2, axis=0), my_slots, slot_total)
    got_queries = lax.all_to_all(send_queries, "mem", split_axis=0, concat_axis=0, tiled=True)
    query_heads = jnp.moveaxis(got_queries.reshape(row_total, head_count, head_width), 1, 0)
    key_heads = jnp.moveaxis(keys.reshape(shard_rows * key_len, head_count, head_width), 1, 0)
    value_heads = jnp.moveaxis(values.reshape(shard_rows * key_len, head_count, head_width), 1, 0)
    row_owner = jnp.repeat(slot_row, token_piece)
    key_owner = jnp.repeat(jnp.arange(shard_rows, dtype=jnp.int32), key_len)
    own_keys = row_owner[:, None] == key_owner[None, :]

    def head_scores(query_one, key_one):
        return (
            jnp.einsum("td,kd->tk", query_one, key_one, preferred_element_type=jnp.float32)
            * scaling
        )

    def forward_head(operands):
        query_one, key_one, value_one = operands
        scores = head_scores(query_one, key_one)
        peak = jnp.max(jnp.where(own_keys, scores, -jnp.inf), axis=1)
        exponent = jnp.where(own_keys, jnp.exp(scores - peak[:, None]), 0.0).astype(jnp.bfloat16)
        norm = jnp.sum(exponent, axis=1, dtype=jnp.float32)
        mix = (
            jnp.einsum("tk,kd->td", exponent, value_one, preferred_element_type=jnp.float32)
            / norm[:, None]
        )
        return (mix, peak, norm)

    head_mix, row_peak, row_norm = lax.map(forward_head, (query_heads, key_heads, value_heads))
    partial_mix = jnp.moveaxis(head_mix, 0, 1)
    back_mix, back_peak, back_norm = (
        lax.all_to_all(
            partial_mix.reshape(slot_total, token_piece, feature_count),
            "mem",
            split_axis=0,
            concat_axis=0,
            tiled=True,
        ),
        lax.all_to_all(
            row_peak.T.reshape(slot_total, token_piece, head_count),
            "mem",
            split_axis=0,
            concat_axis=0,
            tiled=True,
        ),
        lax.all_to_all(
            row_norm.T.reshape(slot_total, token_piece, head_count),
            "mem",
            split_axis=0,
            concat_axis=0,
            tiled=True,
        ),
    )
    part_mix = jnp.take(back_mix, my_slots, axis=0).reshape(
        group_dev, 2, token_piece, head_count, head_width
    )
    part_peak = jnp.take(back_peak, my_slots, axis=0).reshape(group_dev, 2, token_piece, head_count)
    part_norm = jnp.take(back_norm, my_slots, axis=0).reshape(group_dev, 2, token_piece, head_count)
    row_top = jnp.max(part_peak, axis=1)
    weight = jnp.exp(part_peak - row_top[:, None]) * part_norm
    total_norm = jnp.sum(weight, axis=1)
    attended_heads = (jnp.sum(weight[..., None] * part_mix, axis=1) / total_norm[..., None]).astype(
        jnp.bfloat16
    )
    attended = attended_heads.reshape(group_dev, token_piece, feature_count)
    row_dsum = jnp.sum(
        grad_out.reshape(group_dev, token_piece, head_count, head_width).astype(jnp.float32)
        * attended_heads.astype(jnp.float32),
        axis=3,
    )
    send_top = place_rows(jnp.repeat(row_top, 2, axis=0), my_slots, slot_total)
    send_norm = place_rows(jnp.repeat(total_norm, 2, axis=0), my_slots, slot_total)
    send_dsum = place_rows(jnp.repeat(row_dsum, 2, axis=0), my_slots, slot_total)
    got_grads = lax.all_to_all(send_grads, "mem", split_axis=0, concat_axis=0, tiled=True)
    got_top, got_norm, got_dsum = (
        lax.all_to_all(send_top, "mem", split_axis=0, concat_axis=0, tiled=True),
        lax.all_to_all(send_norm, "mem", split_axis=0, concat_axis=0, tiled=True),
        lax.all_to_all(send_dsum, "mem", split_axis=0, concat_axis=0, tiled=True),
    )
    safe_norm = jnp.where(slot_valid[:, None, None], got_norm, 1.0)
    grad_heads = jnp.moveaxis(got_grads.reshape(row_total, head_count, head_width), 1, 0)
    stat_top = got_top.reshape(row_total, head_count).T
    stat_norm = safe_norm.reshape(row_total, head_count).T
    stat_dsum = got_dsum.reshape(row_total, head_count).T

    def backward_head(operands):
        query_one, key_one, value_one, grad_one, top_one, norm_one, dsum_one = operands
        scores = head_scores(query_one, key_one)
        probability = (
            jnp.where(own_keys, jnp.exp(scores - top_one[:, None]), 0.0) / norm_one[:, None]
        )
        prob_half = probability.astype(jnp.bfloat16)
        value_grad = jnp.einsum(
            "tk,td->kd", prob_half, grad_one, preferred_element_type=jnp.float32
        )
        prob_grad = jnp.einsum("td,kd->tk", grad_one, value_one, preferred_element_type=jnp.float32)
        score_half = (probability * (prob_grad - dsum_one[:, None]) * scaling).astype(jnp.bfloat16)
        query_part = jnp.einsum(
            "tk,kd->td", score_half, key_one, preferred_element_type=jnp.float32
        )
        key_grad = jnp.einsum(
            "tk,td->kd", score_half, query_one, preferred_element_type=jnp.float32
        )
        return (query_part, key_grad, value_grad)

    head_query, head_key, head_value = lax.map(
        backward_head,
        (query_heads, key_heads, value_heads, grad_heads, stat_top, stat_norm, stat_dsum),
    )
    query_parts = jnp.moveaxis(head_query, 0, 1)
    key_grads = jnp.moveaxis(head_key, 0, 1)
    value_grads = jnp.moveaxis(head_value, 0, 1)
    returned = lax.all_to_all(
        query_parts.reshape(slot_total, token_piece, feature_count),
        "mem",
        split_axis=0,
        concat_axis=0,
        tiled=True,
    )
    own_grads = jnp.take(returned, my_slots, axis=0).reshape(
        group_dev, 2, token_piece, feature_count
    )
    grad_queries = (own_grads[:, 0] + own_grads[:, 1]).astype(jnp.bfloat16)
    memory_sums = (
        lax.psum_scatter(
            key_grads.reshape(shard_rows, key_len, feature_count),
            "seq",
            scatter_dimension=1,
            tiled=True,
        ),
        lax.psum_scatter(
            value_grads.reshape(shard_rows, key_len, feature_count),
            "seq",
            scatter_dimension=1,
            tiled=True,
        ),
    )
    return (
        attended,
        grad_queries,
        memory_sums[0].astype(jnp.bfloat16),
        memory_sums[1].astype(jnp.bfloat16),
    )


def solution(mesh):
    placed = (
        P("mem", "seq", None),
        P("mem", None, None),
        P("mem", None, None),
        P("mem", "seq", None),
        P(),
        P(),
    )
    return jax.shard_map(
        per_device,
        mesh=mesh,
        in_specs=placed,
        out_specs=(
            P("mem", "seq", None),
            P("mem", "seq", None),
            P("mem", "seq", None),
            P("mem", "seq", None),
        ),
        check_vma=False,
    )
```

profile of v0, /device:TPU:0, one launch (start us, length us, event | category | flops | bytes accessed | tf_op | source)
XLA Modules:
  0.0 814.0 jit_solution(18318656970991013179)
XLA Ops:
  12.0 5.4 scatter_fusion
  17.4 7.4 all-to-all-start
  32.7 62.8 %all-to-all-done = bf16[48,16,2048]{2,1,0:T(8,128)(2,1)S(1)} async-done(((bf16[48,16,2048]{2,1,0:T(8,128)(2,1)}), bf16[48,16,2048]{2,1,0:T(8,128)(2,1)S(1)}, u32[]{:S(2)}, u32[]{:S(2)}) %all-to-all-start) | async-done | bytes 3145760 | tf_op jit(solution)/shard_map/all_to_all | solution.py:47
  102.4 66.3 %while.30 = (s32[]{:T(128)}, f32[16,768,128]{2,1,0:T(8,128)}, f32[16,768]{1,0:T(8,128)S(1)}, f32[16,768]{1,0:T(8,128)S(1)}, bf16[16,768,128]{2,1,0:T(8,128)(2,1)...) while((s32[]{:T(128)}, f32[16,768,128]{2,1,0:T(8,128)}, ...), condition=%wide.region_6.7_spmd.clone, body=%wide.region_3.0_spmd.clone.sunk | while | flops 206928384 | bytes 5628029 | solution.py:73
  174.2 5.8 all-to-all-done.2
  185.7 5.4 scatter_fusion.3
  191.8 6.0 all-to-all-start.6
  214.9 52.0 %all-to-all-done.6 = bf16[48,16,2048]{2,1,0:T(8,128)(2,1)S(1)} async-done(((bf16[48,16,2048]{2,1,0:T(8,128)(2,1)}), bf16[48,16,2048]{2,1,0:T(8,128)(2,1)S(1)}, u32[]{:S(2)}, u32[]{:S(2)}) %all-to-all-start.6) | async-done | bytes 3145760 | tf_op jit(solution)/shard_map/all_to_all | solution.py:118
  270.6 9.0 %copy.40 = f32[768,16,128]{2,1,0:T(8,128)} copy(f32[768,16,128]{2,0,1:T(8,128)} %bitcast.163) | data formatting | bytes 12582912 | tf_op jit(solution)/shard_map/transpose | solution.py:74
  279.6 7.1 reshape.183
  287.3 6.0 all-to-all-start.3
  306.0 125.2 %all-to-all-done.3 = f32[48,16,2048]{2,1,0:T(8,128)} async-done(((f32[48,16,2048]{2,1,0:T(8,128)}), f32[48,16,2048]{2,1,0:T(8,128)}, u32[]{:S(2)}, u32[]{:S(2)}) %all-to-all-start.3) | async-done | bytes 6291488 | tf_op jit(solution)/shard_map/all_to_all | solution.py:76
  435.1 5.7 gather_fusion.2
  452.3 5.9 all-to-all-start.7
  473.2 153.4 %while.31 = (s32[]{:T(128)}, f32[16,768,128]{2,1,0:T(8,128)}, f32[16,512,128]{2,1,0:T(8,128)}, f32[16,512,128]{2,1,0:T(8,128)}, bf16[16,768,128]{2,1,0:T(8,128)(...) while((s32[]{:T(128)}, f32[16,768,128]{2,1,0:T(8,128)}, ...), condition=%wide.region_17.20_spmd.clone, body=%wide.region_16.19_spmd.clone.sunk | while | flops 507248640 | bytes 9214101 | solution.py:150
  626.6 6.6 copy.51
  638.1 9.1 %copy.49 = f32[768,16,128]{2,1,0:T(8,128)} copy(f32[768,16,128]{2,0,1:T(8,128)} %bitcast.162) | data formatting | bytes 12582912 | tf_op jit(solution)/shard_map/transpose | solution.py:154
  647.2 7.4 reshape.193
  654.6 6.0 all-to-all-start.8
  660.8 6.6 copy.50
  674.8 9.1 %reduce-scatter.5.cloned.1.call-done = f32[4,32,2048]{2,1,0:T(8,128)} async-done(((f32[4,128,2048]{2,1,0:T(8,128)}), f32[4,32,2048]{2,1,0:T(8,128)}) %reduce-scatter.5.cloned.1.call-update) | async-done | bytes 1048592 | tf_op jit(solution)/shard_map/reduce_scatter | solution.py:175
  686.0 45.1 %reduce-scatter.3.cloned.1.call-done = f32[4,32,2048]{2,1,0:T(8,128)} async-done(((f32[4,128,2048]{2,1,0:T(8,128)}), f32[4,32,2048]{2,1,0:T(8,128)}) %reduce-scatter.3.cloned.1.call-update) | async-done | bytes 1048592 | tf_op jit(solution)/shard_map/reduce_scatter | solution.py:169
  733.2 64.2 %all-to-all-done.8 = f32[48,16,2048]{2,1,0:T(8,128)} async-done(((f32[48,16,2048]{2,1,0:T(8,128)}), f32[48,16,2048]{2,1,0:T(8,128)}, u32[]{:S(2)}, u32[]{:S(2)}) %all-to-all-start.8) | async-done | bytes 6291488 | tf_op jit(solution)/shard_map/all_to_all | solution.py:157
  797.5 5.8 gather_fusion.3
  (353 shorter events, 334.8 us)
Async XLA Ops:
  8.4 177.3 %copy-start.11 = (s32[32]{0:T(128)}, s32[32]{0:T(128)S(1)}, u32[]{:S(2)}) copy-start(s32[32]{0:T(128)S(1)} %fusion.47) | copy-start | bytes 388
  17.4 7.4 copy-start.15
  17.4 78.1 %all-to-all-start = ((bf16[48,16,2048]{2,1,0:T(8,128)(2,1)}), bf16[48,16,2048]{2,1,0:T(8,128)(2,1)S(1)}, u32[]{:S(2)}, u32[]{:S(2)}) async-start(bf16[48,16,2048]{2,1,0:T(8,128)(2,1)} %scatter_fusion), calls=%async_computation | async-start | bytes 6291456 | tf_op jit(solution)/shard_map/all_to_all | solution.py:47
  28.3 1.9 copy-start.3
  102.4 81.1 %copy-start.1 = (bf16[16,16,2048]{2,1,0:T(8,128)(2,1)S(1)}, bf16[16,16,2048]{2,1,0:T(8,128)(2,1)}, u32[]{:S(2)}) copy-start(bf16[16,16,2048]{2,1,0:T(8,128)(2,1)} %param.17) | copy-start | bytes 3145732
  169.6 10.4 %all-to-all-start.2 = ((f32[8,1,1536]{2,1,0:T(1,128)}), f32[8,1,1536]{2,1,0:T(1,128)S(1)}, u32[]{:S(2)}, u32[]{:S(2)}) async-start(f32[8,1,1536]{2,1,0:T(1,128)} %reshape.285), calls=%async_computation.2 | async-start | bytes 98304 | tf_op jit(solution)/shard_map/all_to_all | solution.py:90
  180.0 11.1 %all-to-all-start.1 = ((f32[8,1,1536]{2,1,0:T(1,128)}), f32[8,1,1536]{2,1,0:T(1,128)S(1)}, u32[]{:S(2)}, u32[]{:S(2)}) async-start(f32[8,1,1536]{2,1,0:T(1,128)} %reshape.287), calls=%async_computation.1 | async-start | bytes 98304 | tf_op jit(solution)/shard_map/all_to_all | solution.py:83
  191.8 75.1 %all-to-all-start.6 = ((bf16[48,16,2048]{2,1,0:T(8,128)(2,1)}), bf16[48,16,2048]{2,1,0:T(8,128)(2,1)S(1)}, u32[]{:S(2)}, u32[]{:S(2)}) async-start(bf16[48,16,2048]{2,1,0:T(8,128)(2,1)} %scatter_fusion.3), calls=%async_computation.6 | async-start | bytes 6291456 | tf_op jit(solution)/shard_map/all_to_all | solution.py:118
  208.5 2.6 copy-start.6
  210.3 0.8 copy-start.4
  266.9 19.7 %all-to-all-start.5 = ((f32[8,1,1536]{2,1,0:T(1,128)}), f32[8,1,1536]{2,1,0:T(1,128)S(1)}, u32[]{:S(2)}, u32[]{:S(2)}) async-start(f32[8,1,1536]{2,1,0:T(1,128)} %reshape.291), calls=%async_computation.5 | async-start | bytes 98304 | tf_op jit(solution)/shard_map/all_to_all | solution.py:121
  286.7 6.6 copy-start.14
  287.3 143.8 %all-to-all-start.3 = ((f32[48,16,2048]{2,1,0:T(8,128)}), f32[48,16,2048]{2,1,0:T(8,128)}, u32[]{:S(2)}, u32[]{:S(2)}) async-start(f32[48,16,2048]{2,1,0:T(8,128)} %reshape.183), calls=%async_computation.3 | async-start | bytes 12582912 | tf_op jit(solution)/shard_map/all_to_all | solution.py:76
  298.1 0.9 copy-start.7
  298.1 1.7 copy-start.12
  431.1 21.2 %all-to-all-start.4 = ((f32[8,1,1536]{2,1,0:T(1,128)}), f32[8,1,1536]{2,1,0:T(1,128)}, u32[]{:S(2)}, u32[]{:S(2)}) async-start(f32[8,1,1536]{2,1,0:T(1,128)} %reshape.289), calls=%async_computation.4 | async-start | bytes 98304 | tf_op jit(solution)/shard_map/all_to_all | solution.py:120
  443.5 1.0 copy-start.8
  444.4 1.6 copy-start
  444.5 1.6 copy-start.5
  452.3 13.7 %all-to-all-start.7 = ((f32[8,1,1536]{2,1,0:T(1,128)}), f32[8,1,1536]{2,1,0:T(1,128)}, u32[]{:S(2)}, u32[]{:S(2)}) async-start(f32[8,1,1536]{2,1,0:T(1,128)} %reshape.293), calls=%async_computation.7 | async-start | bytes 98304 | tf_op jit(solution)/shard_map/all_to_all | solution.py:122
  458.2 225.7 %reduce-scatter.5.cloned.1.call-start = ((), (), s32[]{:S(2)}) async-start(), calls=%async_computation.12 | async-start | bytes 5242880 | tf_op jit(solution)/shard_map/reduce_scatter | solution.py:175
  654.6 142.9 %all-to-all-start.8 = ((f32[48,16,2048]{2,1,0:T(8,128)}), f32[48,16,2048]{2,1,0:T(8,128)}, u32[]{:S(2)}, u32[]{:S(2)}) async-start(f32[48,16,2048]{2,1,0:T(8,128)} %reshape.193), calls=%async_computation.8 | async-start | bytes 12582912 | tf_op jit(solution)/shard_map/all_to_all | solution.py:157
  660.5 70.6 %reduce-scatter.3.cloned.1.call-start = ((), (), s32[]{:S(2)}) async-start(), calls=%async_computation.11 | async-start | bytes 5242880 | tf_op jit(solution)/shard_map/reduce_scatter | solution.py:169
  672.3 1.3 copy-start.2
  (3 other events, 1.8 us)
Sparse Core Ops, SparseCore 0:
  638.2 45.6 reduce-scatter.4
  686.6 44.4 reduce-scatter.2
where the time goes:
time: 821 us; the launch traced here: 814 us
  waiting for transfers between devices  364 us (44%)
  matrix products  186 us (23%)
  local copies, waits for them, and re-layouts  168 us (20%)
  starting transfers between devices  46.4 us (6%)
  other arithmetic  34.1 us (4%)
  between operations  14.4 us (2%)
    all_to_all x1, waiting for transfers between devices, per_device(): lax.all_to_all(partial_mix.reshape(slot_total, token_piece, feature_count...  125 us
    all_to_all x1, waiting for transfers between devices, per_device(): lax.all_to_all(query_parts.reshape(slot_total, token_piece, feature_count...  64.2 us
    all_to_all x1, waiting for transfers between devices, per_device(): lax.all_to_all(send_queries, 'mem', split_axis=0, concat_axis=0, tiled=True)  62.8 us
    all_to_all x1, waiting for transfers between devices, per_device(): lax.all_to_all(send_grads, 'mem', split_axis=0, concat_axis=0, tiled=True)  52 us
    dot_general x32, matrix products, head_scores(): jnp.einsum('td,kd->tk', query_one, key_one, preferred_element_type=jnp.fl...  47.2 us
    reduce_scatter x1, waiting for transfers between devices, per_device(): lax.psum_scatter(key_grads.reshape(shard_rows, key_len, feature_count), '...  45.1 us
    dot_general x16, matrix products, forward_head(): jnp.einsum('tk,kd->td', exponent, value_one, preferred_element_type=jnp.f...  35 us
    dot_general x16, matrix products, backward_head(): jnp.einsum('tk,td->kd', score_half, query_one, preferred_element_type=jnp...  32.7 us
  transfers between devices with their start and end apart: 11, of which 7 were waited for; matrix products, arithmetic and copies ran while one was open for 15% of the time, Pallas kernels for 0%

commit v1 on v0

--- a/solution.py
+++ b/solution.py
@@ -5,6 +5,18 @@
 from jax.sharding import PartitionSpec as P
 
 HEADS = 16
+
+
+def exchange_directly(value, axis, split, join):
+    ways, here = (lax.axis_size(axis), lax.axis_index(axis))
+    width = value.shape[split] // ways
+    turned = jnp.roll(value, -here * width, axis=split)
+    got = [lax.slice_in_dim(turned, 0, width, axis=split)]
+    for far in range(1, ways):
+        sent = lax.slice_in_dim(turned, far * width, (far + 1) * width, axis=split)
+        got.append(lax.ppermute(sent, axis, [(d, (d + far) % ways) for d in range(ways)]))
+    line = jnp.concatenate(got[::-1], axis=join)
+    return jnp.roll(line, (here + 1) * got[0].shape[join], axis=join)
 
 
 def route_tables(owners, shard_cap):
@@ -154,12 +166,8 @@
     query_parts = jnp.moveaxis(head_query, 0, 1)
     key_grads = jnp.moveaxis(head_key, 0, 1)
     value_grads = jnp.moveaxis(head_value, 0, 1)
-    returned = lax.all_to_all(
-        query_parts.reshape(slot_total, token_piece, feature_count),
-        "mem",
-        split_axis=0,
-        concat_axis=0,
-        tiled=True,
+    returned = exchange_directly(
+        query_parts.reshape(slot_total, token_piece, feature_count), "mem", 0, 0
     )
     own_grads = jnp.take(returned, my_slots, axis=0).reshape(
         group_dev, 2, token_piece, feature_count

time: 821 us -> 895 us (1.090)
  local copies, waits for them, and re-layouts: 168 us -> 214 us
  waiting for transfers between devices: 364 us -> 375 us
    ppermute x0 -> x7, waiting for transfers between devices: none -> 128 us  [exchange_directly(): lax.ppermute(sent, axis, [(d, (d + far) % ways) for d in range(ways)])]
    all_to_all x1 -> x0, waiting for transfers between devices: 64.2 us -> none  [per_device(): lax.all_to_all(query_parts.reshape(slot_total, token_piece, feature_count...]
    reduce_scatter x1, waiting for transfers between devices: 45.1 us -> 0.01 us  [per_device(): lax.psum_scatter(key_grads.reshape(shard_rows, key_len, feature_count), '...]
    dynamic_update_slice x32, local copies, waits for them, and re-layouts: 2.8 us -> 43.6 us  [per_device(): lax.map(forward_head, (query_heads, key_heads, value_heads))]
    concatenate x0 -> x2, other arithmetic: none -> 9.64 us  [the longest x1 4.97 us: exchange_directly(): return jnp.roll(line, (here + 1) * got[0].shape[join], axis=join)]
    reduce_scatter x1, waiting for transfers between devices: 9.08 us -> 0.01 us  [per_device(): lax.psum_scatter(value_grads.reshape(shard_rows, key_len, feature_count),...]
    unnamed x54 -> x65, local copies, waits for them, and re-layouts: 29.4 us -> 28.6 us
  transfers between devices with their start and end apart: 11 -> 17, of which waited for: 7 -> 10; matrix products, arithmetic and copies ran while one was open for 15% -> 16% of each run, Pallas kernels for 0% -> 0%
where the time goes in v1:
time: 895 us; the launch traced here: 879 us
  waiting for transfers between devices  375 us (42%)
  local copies, waits for them, and re-layouts  214 us (24%)
  matrix products  184 us (21%)
  starting transfers between devices  48.5 us (5%)
  other arithmetic  41.6 us (5%)
  between operations  15.1 us (2%)
    ppermute x7, waiting for transfers between devices, exchange_directly(): lax.ppermute(sent, axis, [(d, (d + far) % ways) for d in range(ways)])  128 us
    all_to_all x1, waiting for transfers between devices, per_device(): lax.all_to_all(partial_mix.reshape(slot_total, token_piece, feature_count...  125 us
    all_to_all x1, waiting for transfers between devices, per_device(): lax.all_to_all(send_queries, 'mem', split_axis=0, concat_axis=0, tiled=True)  62.7 us
    all_to_all x1, waiting for transfers between devices, per_device(): lax.all_to_all(send_grads, 'mem', split_axis=0, concat_axis=0, tiled=True)  53.2 us
    dot_general x32, matrix products, head_scores(): jnp.einsum('td,kd->tk', query_one, key_one, preferred_element_type=jnp.fl...  45.7 us
    dynamic_update_slice x32, local copies, waits for them, and re-layouts, per_device(): lax.map(forward_head, (query_heads, key_heads, value_heads))  43.6 us
    dot_general x16, matrix products, forward_head(): jnp.einsum('tk,kd->td', exponent, value_one, preferred_element_type=jnp.f...  35 us
    dot_general x16, matrix products, backward_head(): jnp.einsum('tk,td->kd', score_half, query_one, preferred_element_type=jnp...  32.6 us
  transfers between devices with their start and end apart: 17, of which 10 were waited for; matrix products, arithmetic and copies ran while one was open for 16% of the time, Pallas kernels for 0%

profile of v1, /device:TPU:0, one launch (start us, length us, event | category | flops | bytes accessed | tf_op | source)
XLA Modules:
  0.0 879.2 jit_solution(9280698889937461215)
XLA Ops:
  12.0 5.4 scatter_fusion
  17.4 7.4 all-to-all-start
  32.7 62.7 %all-to-all-done = bf16[48,16,2048]{2,1,0:T(8,128)(2,1)S(1)} async-done(((bf16[48,16,2048]{2,1,0:T(8,128)(2,1)}), bf16[48,16,2048]{2,1,0:T(8,128)(2,1)S(1)}, u32[]{:S(2)}, u32[]{:S(2)}) %all-to-all-start) | async-done | bytes 3145760 | tf_op jit(solution)/shard_map/all_to_all | solution.py:59
  100.6 105.0 %while.30 = (s32[]{:T(128)}, f32[16,768,128]{2,1,0:T(8,128)}, f32[16,768]{1,0:T(8,128)}, f32[16,768]{1,0:T(8,128)}, bf16[16,768,128]{2,1,0:T(8,128)(2,1)S(1)}, /...) while((s32[]{:T(128)}, f32[16,768,128]{2,1,0:T(8,128)}, ...), condition=%wide.region_6.7_spmd.clone, body=%wide.region_3.0_spmd.clone.sunk | while | flops 206928384 | bytes 5629045 | solution.py:85
  225.1 5.4 scatter_fusion.3
  230.5 6.0 all-to-all-start.6
  252.2 53.2 %all-to-all-done.6 = bf16[48,16,2048]{2,1,0:T(8,128)(2,1)S(1)} async-done(((bf16[48,16,2048]{2,1,0:T(8,128)(2,1)}), bf16[48,16,2048]{2,1,0:T(8,128)(2,1)S(1)}, u32[]{:S(2)}, u32[]{:S(2)}) %all-to-all-start.6) | async-done | bytes 3145760 | tf_op jit(solution)/shard_map/all_to_all | solution.py:130
  309.2 9.1 %copy.40 = f32[768,16,128]{2,1,0:T(8,128)} copy(f32[768,16,128]{2,0,1:T(8,128)} %bitcast.158) | data formatting | bytes 12582912 | tf_op jit(solution)/shard_map/transpose | solution.py:86
  318.3 7.1 reshape.183
  326.0 6.0 all-to-all-start.3
  344.7 125.2 %all-to-all-done.3 = f32[48,16,2048]{2,1,0:T(8,128)} async-done(((f32[48,16,2048]{2,1,0:T(8,128)}), f32[48,16,2048]{2,1,0:T(8,128)}, u32[]{:S(2)}, u32[]{:S(2)}) %all-to-all-start.3) | async-done | bytes 6291488 | tf_op jit(solution)/shard_map/all_to_all | solution.py:88
  473.8 5.8 gather_fusion.2
  491.0 5.9 all-to-all-start.7
  511.0 153.4 %while.31 = (s32[]{:T(128)}, f32[16,768,128]{2,1,0:T(8,128)}, f32[16,512,128]{2,1,0:T(8,128)}, f32[16,512,128]{2,1,0:T(8,128)}, bf16[16,768,128]{2,1,0:T(8,128)(...) while((s32[]{:T(128)}, f32[16,768,128]{2,1,0:T(8,128)}, ...), condition=%wide.region_17.20_spmd.clone, body=%wide.region_16.19_spmd.clone.sunk | while | flops 507248640 | bytes 9214093 | solution.py:162
  664.4 6.7 copy.50
  676.0 6.7 copy.51
  682.7 5.2 reshape.196
  688.0 9.1 %copy.49 = f32[768,16,128]{2,1,0:T(8,128)} copy(f32[768,16,128]{2,0,1:T(8,128)} %bitcast.157) | data formatting | bytes 12582912 | tf_op jit(solution)/shard_map/transpose | solution.py:166
  697.1 7.1 reshape.193
  722.0 13.6 %collective-permute-done = f32[6,16,2048]{2,1,0:T(8,128)} collective-permute-done((f32[6,16,2048]{2,1,0:T(8,128)}, f32[6,16,2048]{2,1,0:T(8,128)}, u32[]{:S(2)}, u32[]{:S(2)}) %collective-permute-start) | collective-permute-done | bytes 786464 | tf_op jit(solution)/shard_map/ppermute | solution.py:17
  736.8 15.7 %collective-permute-done.1 = f32[6,16,2048]{2,1,0:T(8,128)S(1)} collective-permute-done((f32[6,16,2048]{2,1,0:T(8,128)}, f32[6,16,2048]{2,1,0:T(8,128)S(1)}, u32[]{:S(2)}, u32[]{:S(2)}) %collective-permute-start.1) | collective-permute-done | bytes 786464 | tf_op jit(solution)/shard_map/ppermute | solution.py:17
  752.8 16.6 %collective-permute-done.2 = f32[6,16,2048]{2,1,0:T(8,128)S(1)} collective-permute-done((f32[6,16,2048]{2,1,0:T(8,128)}, f32[6,16,2048]{2,1,0:T(8,128)S(1)}, u32[]{:S(2)}, u32[]{:S(2)}) %collective-permute-start.2) | collective-permute-done | bytes 786464 | tf_op jit(solution)/shard_map/ppermute | solution.py:17
  769.5 82.0 %collective-permute-done.3 = f32[6,16,2048]{2,1,0:T(8,128)S(1)} collective-permute-done((f32[6,16,2048]{2,1,0:T(8,128)}, f32[6,16,2048]{2,1,0:T(8,128)S(1)}, u32[]{:S(2)}, u32[]{:S(2)}) %collective-permute-start.3) | collective-permute-done | bytes 786464 | tf_op jit(solution)/shard_map/ppermute | solution.py:17
  858.1 5.8 gather_fusion.3
  (380 shorter events, 396.0 us)
Async XLA Ops:
  8.4 3.6 copy-start.16
  8.4 216.7 %copy-start.11 = (s32[32]{0:T(128)}, s32[32]{0:T(128)S(1)}, u32[]{:S(2)}) copy-start(s32[32]{0:T(128)S(1)} %fusion.49) | copy-start | bytes 388
  17.4 7.4 copy-start.17
  17.4 78.1 %all-to-all-start = ((bf16[48,16,2048]{2,1,0:T(8,128)(2,1)}), bf16[48,16,2048]{2,1,0:T(8,128)(2,1)S(1)}, u32[]{:S(2)}, u32[]{:S(2)}) async-start(bf16[48,16,2048]{2,1,0:T(8,128)(2,1)} %scatter_fusion), calls=%async_computation | async-start | bytes 6291456 | tf_op jit(solution)/shard_map/all_to_all | solution.py:59
  205.6 12.6 %copy-start.2 = (bf16[16,768,128]{2,1,0:T(8,128)(2,1)}, bf16[16,768,128]{2,1,0:T(8,128)(2,1)S(1)}, u32[]{:S(2)}) copy-start(bf16[16,768,128]{2,1,0:T(8,128)(2,1)S(1)} %get-tuple-element.505) | copy-start | bytes 9437188
  207.4 10.8 %all-to-all-start.1 = ((f32[8,1,1536]{2,1,0:T(1,128)}), f32[8,1,1536]{2,1,0:T(1,128)}, u32[]{:S(2)}, u32[]{:S(2)}) async-start(f32[8,1,1536]{2,1,0:T(1,128)} %reshape.287), calls=%async_computation.1 | async-start | bytes 98304 | tf_op jit(solution)/shard_map/all_to_all | solution.py:95
  218.2 12.3 %all-to-all-start.2 = ((f32[8,1,1536]{2,1,0:T(1,128)}), f32[8,1,1536]{2,1,0:T(1,128)S(1)}, u32[]{:S(2)}, u32[]{:S(2)}) async-start(f32[8,1,1536]{2,1,0:T(1,128)} %reshape.285), calls=%async_computation.2 | async-start | bytes 98304 | tf_op jit(solution)/shard_map/all_to_all | solution.py:102
  230.5 74.9 %all-to-all-start.6 = ((bf16[48,16,2048]{2,1,0:T(8,128)(2,1)}), bf16[48,16,2048]{2,1,0:T(8,128)(2,1)S(1)}, u32[]{:S(2)}, u32[]{:S(2)}) async-start(bf16[48,16,2048]{2,1,0:T(8,128)(2,1)} %scatter_fusion.3), calls=%async_computation.6 | async-start | bytes 6291456 | tf_op jit(solution)/shard_map/all_to_all | solution.py:130
  237.1 11.2 %copy-start.13 = (s32[1024]{0:T(1024)}, s32[1024]{0:T(1024)S(1)}, u32[]{:S(2)}) copy-start(s32[1024]{0:T(1024)S(1)} %pad_clamp_fusion) | copy-start | bytes 12292
  305.4 20.0 %all-to-all-start.5 = ((f32[8,1,1536]{2,1,0:T(1,128)}), f32[8,1,1536]{2,1,0:T(1,128)S(1)}, u32[]{:S(2)}, u32[]{:S(2)}) async-start(f32[8,1,1536]{2,1,0:T(1,128)} %reshape.291), calls=%async_computation.5 | async-start | bytes 98304 | tf_op jit(solution)/shard_map/all_to_all | solution.py:133
  326.0 143.8 %all-to-all-start.3 = ((f32[48,16,2048]{2,1,0:T(8,128)}), f32[48,16,2048]{2,1,0:T(8,128)}, u32[]{:S(2)}, u32[]{:S(2)}) async-start(f32[48,16,2048]{2,1,0:T(8,128)} %reshape.183), calls=%async_computation.3 | async-start | bytes 12582912 | tf_op jit(solution)/shard_map/all_to_all | solution.py:88
  469.8 21.2 %all-to-all-start.4 = ((f32[8,1,1536]{2,1,0:T(1,128)}), f32[8,1,1536]{2,1,0:T(1,128)}, u32[]{:S(2)}, u32[]{:S(2)}) async-start(f32[8,1,1536]{2,1,0:T(1,128)} %reshape.289), calls=%async_computation.4 | async-start | bytes 98304 | tf_op jit(solution)/shard_map/all_to_all | solution.py:132
  491.0 12.8 %all-to-all-start.7 = ((f32[8,1,1536]{2,1,0:T(1,128)}), f32[8,1,1536]{2,1,0:T(1,128)}, u32[]{:S(2)}, u32[]{:S(2)}) async-start(f32[8,1,1536]{2,1,0:T(1,128)} %reshape.293), calls=%async_computation.7 | async-start | bytes 98304 | tf_op jit(solution)/shard_map/all_to_all | solution.py:134
  496.9 370.8 %reduce-scatter.3.cloned.1.call-start = ((), (), s32[]{:S(2)}) async-start(), calls=%async_computation.10 | async-start | bytes 5242880 | tf_op jit(solution)/shard_map/reduce_scatter | solution.py:177
  675.9 193.9 %reduce-scatter.5.cloned.1.call-start = ((), (), s32[]{:S(2)}) async-start(), calls=%async_computation.11 | async-start | bytes 5242880 | tf_op jit(solution)/shard_map/reduce_scatter | solution.py:183
  708.9 4.3 copy-start
  708.9 11.9 %copy-start.3 = (bf16[16,16,16,128]{3,2,1,0:T(8,128)(2,1)S(1)}, bf16[16,16,16,128]{3,2,1,0:T(8,128)(2,1)}, u32[]{:S(2)}) copy-start(bf16[16,16,16,128]{3,2,1,0:T(8,128)(2,1)} %get-tuple-element.262) | copy-start | bytes 3145732
  713.2 22.5 %collective-permute-start = (f32[6,16,2048]{2,1,0:T(8,128)}, f32[6,16,2048]{2,1,0:T(8,128)}, u32[]{:S(2)}, u32[]{:S(2)}) collective-permute-start(f32[6,16,2048]{2,1,0:T(8,128)} %get-tuple-element.277), channel_id=1, source_target_pairs={{0,7},{1,0},{2,1},{3,2},{4,3},{5,4},{6,5},{7,6},{8,15},{9,8},{10,9... | collective-permute-start | bytes 2359304 | tf_op jit(solution)/shard_map/ppermute | solution.py:17
  717.3 35.2 %collective-permute-start.1 = (f32[6,16,2048]{2,1,0:T(8,128)}, f32[6,16,2048]{2,1,0:T(8,128)S(1)}, u32[]{:S(2)}, u32[]{:S(2)}) collective-permute-start(f32[6,16,2048]{2,1,0:T(8,128)} %get-tuple-element.276), channel_id=1, source_target_pairs={{0,6},{1,7},{2,0},{3,1},{4,2},{5,3},{6,4},{7,5},{8,14},{9,15},{10,... | collective-permute-start | bytes 2359304 | tf_op jit(solution)/shard_map/ppermute | solution.py:17
  717.9 51.5 %collective-permute-start.2 = (f32[6,16,2048]{2,1,0:T(8,128)}, f32[6,16,2048]{2,1,0:T(8,128)S(1)}, u32[]{:S(2)}, u32[]{:S(2)}) collective-permute-start(f32[6,16,2048]{2,1,0:T(8,128)} %get-tuple-element.275), channel_id=1, source_target_pairs={{0,5},{1,6},{2,7},{3,0},{4,1},{5,2},{6,3},{7,4},{8,13},{9,14},{10,... | collective-permute-start | bytes 2359304 | tf_op jit(solution)/shard_map/ppermute | solution.py:17
  717.9 133.6 %collective-permute-start.3 = (f32[6,16,2048]{2,1,0:T(8,128)}, f32[6,16,2048]{2,1,0:T(8,128)S(1)}, u32[]{:S(2)}, u32[]{:S(2)}) collective-permute-start(f32[6,16,2048]{2,1,0:T(8,128)} %get-tuple-element.274), channel_id=1, source_target_pairs={{0,4},{1,5},{2,6},{3,7},{4,0},{5,1},{6,2},{7,3},{8,12},{9,13},{10,... | collective-permute-start | bytes 2359304 | tf_op jit(solution)/shard_map/ppermute | solution.py:17
  722.0 129.7 %collective-permute-start.4 = (f32[6,16,2048]{2,1,0:T(8,128)}, f32[6,16,2048]{2,1,0:T(8,128)S(1)}, u32[]{:S(2)}, u32[]{:S(2)}) collective-permute-start(f32[6,16,2048]{2,1,0:T(8,128)} %get-tuple-element.273), channel_id=1, source_target_pairs={{0,3},{1,4},{2,5},{3,6},{4,7},{5,0},{6,1},{7,2},{8,11},{9,12},{10,... | collective-permute-start | bytes 2359304 | tf_op jit(solution)/shard_map/ppermute | solution.py:17
  735.7 116.1 %collective-permute-start.5 = (f32[6,16,2048]{2,1,0:T(8,128)}, f32[6,16,2048]{2,1,0:T(8,128)S(1)}, u32[]{:S(2)}, u32[]{:S(2)}) collective-permute-start(f32[6,16,2048]{2,1,0:T(8,128)} %get-tuple-element.272), channel_id=1, source_target_pairs={{0,2},{1,3},{2,4},{3,5},{4,6},{5,7},{6,0},{7,1},{8,10},{9,11},{10,... | collective-permute-start | bytes 2359304 | tf_op jit(solution)/shard_map/ppermute | solution.py:17
  752.5 99.3 %collective-permute-start.6 = (f32[6,16,2048]{2,1,0:T(8,128)}, f32[6,16,2048]{2,1,0:T(8,128)S(1)}, u32[]{:S(2)}, u32[]{:S(2)}) collective-permute-start(f32[6,16,2048]{2,1,0:T(8,128)} %get-tuple-element.271), channel_id=1, source_target_pairs={{0,1},{1,2},{2,3},{3,4},{4,5},{5,6},{6,7},{7,0},{8,9},{9,10},{10,1... | collective-permute-start | bytes 2359304 | tf_op jit(solution)/shard_map/ppermute | solution.py:17
  (11 other events, 16.2 us)
Sparse Core Ops, SparseCore 0:
  676.1 45.0 reduce-scatter.2
  723.8 44.4 reduce-scatter.4
